TPU v7x, 768 devices: a whole 4x8x12 slice. The times are simulated.
768 devices in a mesh: tab: 8 (over x, core), rep: 96 (over z, y).
Axes of the slice: x: 4, y: 8, z: 12, core: 2. Of those that a mesh axis runs over, the one named last changes fastest.
Arguments:
- d_proj: bfloat16 [96, 1024, 8, 256], P('rep', 'tab'), may hold values from -6 to 6
- pooled: bfloat16 [96, 1024, 8, 512], P('rep', 'tab'), may hold values from -6 to 6
- proj: bfloat16 [8, 512, 256], replicated, may hold values from -0.25 to 0.25
- bag_rows: int32 [96, 1024, 8, 8], P('rep', None, 'tab'), may hold values from 0 to 511
- bag_lengths: int32 [96, 1024, 8], P('rep', None, 'tab'), may hold values from 1 to 8
- dim_blocks: int32 [8], replicated, may hold values from 1 to 16
Outputs:
- emb_grad: float32 [8, 512, 512], P('tab')
- proj_grad: float32 [8, 512, 256], P('tab')
All inputs are finite; a program needn't handle non-finite values.
Results may differ from a plain program's by a relative error of at most 0.003.
Values may be sent and summed in bfloat16 or wider, within the bound.
No kernel may reach another device: no remote copies, remote signals or barrier semaphores. Data moves between devices by JAX's collectives and lax.ppermute only.
A program may use at most 32 MiB of HBM per device.

v0:
```python
import jax
import jax.numpy as jnp
from jax import lax
from jax.sharding import PartitionSpec as P

ROWS = 512


def body(d_proj, pooled, proj, bag_rows, bag_lengths, dim_blocks):
    widest = proj.shape[1]
    group_rows = bag_rows.shape[1]
    bag_size = bag_rows.shape[3]
    columns = jnp.arange(widest, dtype=jnp.int32)
    live = (columns[None, :] < (widest // 16 * dim_blocks)[:, None]).astype(jnp.float32)
    samples_proj = d_proj[0]
    masked_pool = jnp.where(live[None, :, :] > 0, pooled[0], jnp.zeros_like(pooled[0]))
    proj_part = lax.psum_scatter(
        jnp.einsum("bte,btp->tep", masked_pool, samples_proj, preferred_element_type=jnp.float32),
        "tab",
        scatter_dimension=0,
        tiled=True,
    )
    back = jnp.einsum("btp,tep->bte", samples_proj, proj, preferred_element_type=jnp.float32)
    back = (back * live[None, :, :]).astype(jnp.bfloat16)
    d_pooled = lax.all_to_all(back, "tab", split_axis=1, concat_axis=0, tiled=True)
    row_count = ROWS
    row_ids = jnp.arange(row_count, dtype=jnp.int32)
    counts = jnp.zeros((group_rows, row_count), jnp.float32)
    for slot in range(bag_size):
        hit = (bag_rows[0, :, 0, slot][:, None] == row_ids[None, :]) & (
            slot < bag_lengths[0, :, 0]
        )[:, None]
        counts = counts + hit.astype(jnp.float32)
    grads = [
        lax.dot_general(
            counts.astype(jnp.bfloat16),
            d_pooled[:, 0, :],
            (((0,), (0,)), ((), ())),
            preferred_element_type=jnp.float32,
        )
    ]
    emb_part = jnp.stack(grads, axis=0)
    emb_grad, proj_grad = lax.psum((emb_part, proj_part), "rep")
    return (emb_grad, proj_grad)


def solution(mesh):
    placed = (
        P("rep", "tab", None, None),
        P("rep", "tab", None, None),
        P(),
        P("rep", None, "tab", None),
        P("rep", None, "tab"),
        P(),
    )
    return jax.shard_map(
        body,
        mesh=mesh,
        in_specs=placed,
        out_specs=(P("tab", None, None), P("tab", None, None)),
        check_vma=False,
    )
```

profile of v0, /device:TPU:2, one launch (start us, length us, event | category | flops | bytes accessed | tf_op | source)
XLA Modules:
  0.0 320.6 jit_solution(16083346748950771666)
XLA Ops:
  7.2 0.0 copy-start
  7.2 0.0 copy-start.2
  7.2 0.0 reduce-scatter.2.cloned.1.call-start
  7.2 0.8 broadcast_multiply_fusion
  8.1 0.1 broadcast_compare_fusion
  8.2 1.3 bitcast_select_fusion
  9.4 0.0 copy-done.2
  9.5 2.7 fusion.9
  12.2 0.0 reduce-scatter.2.cloned.1.call-update
  12.2 0.0 copy-done
  12.2 0.0 copy-start.4
  12.2 0.0 copy-start.3
  12.2 1.8 fusion.8
  14.0 13.0 %all-to-all-start = ((bf16[128,8,512]{0,2,1:T(8,128)(2,1)}), bf16[128,8,512]{0,2,1:T(8,128)(2,1)S(1)}, u32[]{:S(2)}, u32[]{:S(2)}) async-start(bf16[128,8,512]{0,2,1:T(8,128)(2,1)} %fusion.8), calls=%async_computation | async-start | bytes 2097152 | tf_op jit(solution)/shard_map/all_to_all | solution.py:25
  27.0 0.0 all-reduce.3.cloned.1.call-start
  27.0 0.0 copy-done.4
  27.0 0.1 compare_reduce_fusion.7
  27.1 0.0 copy-done.3
  27.2 16.0 %all-to-all-done = bf16[128,8,512]{0,2,1:T(8,128)(2,1)S(1)} async-done(((bf16[128,8,512]{0,2,1:T(8,128)(2,1)}), bf16[128,8,512]{0,2,1:T(8,128)(2,1)S(1)}, u32[]{:S(2)}, u32[]{:S(2)}) %all-to-all-start) | async-done | bytes 1048608 | tf_op jit(solution)/shard_map/all_to_all | solution.py:25
  43.2 1.3 copy.12
  44.5 5.9 %convolution_bitcast_fusion = f32[1,512,512]{2,1,0:T(8,128)} fusion(bf16[1024,512]{1,0:T(8,128)(2,1)} %bitcast.22, s32[1024]{0:T(1024)S(1)} %bitcast.31, s32[1024]{0:T(1024)S(1)} %bitcast.32, s32[1024]{0:T(1024)S(1)} %bitcast.26, s32[1024]{0:T(1024)S(1)} %bitcast.27, s32[1024]{0:T(1024)S(1)} %bitcast.28, s32[1024]{0:T(1024)S(1)} %bitcast.29, ...), kind=kOutput, calls=%fused_computation.19 | convolution fusion | flops 553648128 | bytes 2138112 | tf_op jit(solution)/shard_map/dot_general | solution.py:35
  50.4 14.4 %reduce-scatter.2.cloned.1.call-done = f32[1,512,256]{2,1,0:T(8,128)} async-done(((f32[8,512,256]{2,1,0:T(8,128)}), f32[1,512,256]{2,1,0:T(8,128)}) %reduce-scatter.2.cloned.1.call-update) | async-done | bytes 524304 | tf_op jit(solution)/shard_map/reduce_scatter | solution.py:17
  64.8 0.0 all-reduce.3.cloned.1.call-update
  64.8 245.8 %all-reduce.3.cloned.1.call-done = (f32[1,512,512]{2,1,0:T(8,128)}, f32[1,512,256]{2,1,0:T(8,128)}) async-done(((f32[1,512,512]{2,1,0:T(8,128)}, f32[1,512,256]{2,1,0:T(8,128)}), (f32[1,512,512]{2,1,0:T(8,128)}, f32[1,512,256]{2,1,0:T(8,128)})) %all-reduce.3.cloned.1.call-update) | async-done | bytes 1572880 | tf_op jit(solution)/shard_map/psum | solution.py:43
  310.6 0.0 copy-start.1
  310.6 2.3 copy.23
  313.0 0.0 copy-done.1
  313.0 0.8 copy.24
  (1 shorter events, 0.0 us)
Async XLA Ops:
  7.2 5.0 %copy-start = (bf16[8,512,256]{2,1,0:T(8,128)(2,1)S(1)}, bf16[8,512,256]{2,1,0:T(8,128)(2,1)}, u32[]{:S(2)}) copy-start(bf16[8,512,256]{2,1,0:T(8,128)(2,1)} %param.8) | copy-start | bytes 6291460
  7.2 2.3 copy-start.2
  7.2 57.6 %reduce-scatter.2.cloned.1.call-start = ((), (), s32[]{:S(2)}) async-start(), calls=%async_computation.2 | async-start | bytes 4718592 | tf_op jit(solution)/shard_map/reduce_scatter | solution.py:17
  12.2 14.8 %copy-start.4 = (s32[1,1024,1]{1,2,0:T(1,128)S(1)}, s32[1,1024,1]{1,2,0:T(1,128)}, u32[]{:S(2)}) copy-start(s32[1,1024,1]{1,2,0:T(1,128)} %param.10) | copy-start | bytes 12292
  12.2 14.9 %copy-start.3 = (s32[1,1024,1,8]{1,3,2,0:T(8,128)S(1)}, s32[1,1024,1,8]{1,3,2,0:T(8,128)}, u32[]{:S(2)}) copy-start(s32[1,1024,1,8]{1,3,2,0:T(8,128)} %param.9) | copy-start | bytes 98308
  14.0 29.2 %all-to-all-start = ((bf16[128,8,512]{0,2,1:T(8,128)(2,1)}), bf16[128,8,512]{0,2,1:T(8,128)(2,1)S(1)}, u32[]{:S(2)}, u32[]{:S(2)}) async-start(bf16[128,8,512]{0,2,1:T(8,128)(2,1)} %fusion.8), calls=%async_computation | async-start | bytes 2097152 | tf_op jit(solution)/shard_map/all_to_all | solution.py:25
  27.0 283.6 %all-reduce.3.cloned.1.call-start = ((), (), s32[]{:S(2)}) async-start(), calls=%async_computation.3 | async-start | bytes 3145728 | tf_op jit(solution)/shard_map/psum | solution.py:43
  310.6 2.3 copy-start.1
Sparse Core Ops, SparseCore 0:
  12.3 52.4 reduce-scatter.1
  68.7 241.9 all-reduce.2
where the time goes:
time: 321 us
  waiting for transfers between devices  276 us (86%)
  between operations  14.1 us (4%)
  starting transfers between devices  13.1 us (4%)
  matrix products  10.4 us (3%)
  local copies, waits for them, and re-layouts  4.47 us (1%)
    psum x1, waiting for transfers between devices, body(): emb_grad, proj_grad = lax.psum((emb_part, proj_part), 'rep')  246 us
    all_to_all x1, waiting for transfers between devices, body(): lax.all_to_all(back, 'tab', split_axis=1, concat_axis=0, tiled=True)  16 us
    reduce_scatter x1, waiting for transfers between devices, body(): lax.psum_scatter(jnp.einsum('bte,btp->tep', masked_pool, samples_proj, pr...  14.4 us
    all_to_all x1, starting transfers between devices, body(): lax.all_to_all(back, 'tab', split_axis=1, concat_axis=0, tiled=True)  13 us
  transfers between devices with their start and end apart: 3, of which 3 were waited for; matrix products, arithmetic and copies ran while one was open for 3% of the time, Pallas kernels for 0%

commit v1 on v0

v1 whole, which is shorter than its diff:
```python
import jax
import jax.numpy as jnp
from jax import lax
from jax.sharding import PartitionSpec as P

ROWS = 512
LANES = 128
SUBLANES = 8
WIRE = jnp.float16


def stack_halves(part):
    return [part[:, at : at + LANES] for at in range(0, part.shape[1], LANES)]


def body(d_proj, pooled, proj, bag_rows, bag_lengths, dim_blocks):
    tables, widest, width = proj.shape
    group_rows = bag_rows.shape[1]
    bag_size = bag_rows.shape[3]
    peers = lax.axis_size("rep")
    table = lax.axis_index("tab")

    samples = lax.all_to_all(jnp.swapaxes(d_proj[0], 0, 1), "tab", 0, 0, tiled=True)
    samples = samples.reshape(group_rows, width)
    pools = lax.all_to_all(jnp.swapaxes(pooled[0], 0, 1), "tab", 0, 0, tiled=True)
    pools = pools.reshape(group_rows, widest)

    row_ids = jnp.arange(ROWS, dtype=jnp.int32)
    counts = jnp.zeros((ROWS, group_rows), jnp.float32)
    for slot in range(bag_size):
        hit = (bag_rows[0, :, 0, slot][None, :] == row_ids[:, None]) & (
            slot < bag_lengths[0, :, 0]
        )[None, :]
        counts = counts + hit.astype(jnp.float32)
    row_sums = jnp.dot(counts.astype(jnp.bfloat16), samples, preferred_element_type=jnp.float32)
    outer = lax.dot_general(
        pools, samples, (((0,), (0,)), ((), ())), preferred_element_type=jnp.float32
    )

    pieces = stack_halves(row_sums) + stack_halves(outer)
    rows = sum(piece.shape[0] for piece in pieces)
    share = -(-rows // (peers * SUBLANES)) * SUBLANES
    pad = jnp.zeros((share * peers - rows, LANES), WIRE)
    flat = jnp.concatenate([piece.astype(WIRE) for piece in pieces] + [pad], axis=0)
    parts = lax.all_to_all(flat.reshape(peers, share, LANES), "rep", 0, 0, tiled=True)
    total = jnp.sum(parts.astype(jnp.float32), axis=0)

    mine = jnp.broadcast_to((total * (1.0 / 128.0)).astype(WIRE)[None], (peers, share, LANES))
    full = lax.all_to_all(mine, "rep", 0, 0, tiled=True).reshape(peers * share, LANES)
    full = full.astype(jnp.float32) * 128.0
    half = width // LANES
    row_total = jnp.concatenate([full[i * ROWS : (i + 1) * ROWS] for i in range(half)], axis=1)
    base = half * ROWS
    proj_grad = jnp.concatenate(
        [full[base + i * widest : base + (i + 1) * widest] for i in range(half)], axis=1
    )

    limit = widest // 16 * lax.dynamic_index_in_dim(dim_blocks, table, 0, keepdims=False)
    live = jnp.arange(widest, dtype=jnp.int32) < limit
    weight = lax.dynamic_index_in_dim(proj, table, 0, keepdims=False)
    weight = jnp.where(live[:, None], weight, jnp.zeros_like(weight))
    high = row_total.astype(jnp.bfloat16)
    low = (row_total - high.astype(jnp.float32)).astype(jnp.bfloat16)
    emb_grad = lax.dot_general(
        high, weight, (((1,), (1,)), ((), ())), preferred_element_type=jnp.float32
    ) + lax.dot_general(low, weight, (((1,), (1,)), ((), ())), preferred_element_type=jnp.float32)
    proj_grad = jnp.where(live[:, None], proj_grad, 0.0)
    return (emb_grad[None], proj_grad[None])


def solution(mesh):
    placed = (
        P("rep", "tab", None, None),
        P("rep", "tab", None, None),
        P(),
        P("rep", None, "tab", None),
        P("rep", None, "tab"),
        P(),
    )
    return jax.shard_map(
        body,
        mesh=mesh,
        in_specs=placed,
        out_specs=(P("tab", None, None), P("tab", None, None)),
        check_vma=False,
    )
```

time: 321 us -> 129 us (0.40)
  the two profiles are of different devices: /device:TPU:2 before, /device:TPU:8 now
where the time goes in v1:
time: 129 us
  blocking collectives  50.7 us (39%)
  waiting for transfers between devices  47.9 us (37%)
  starting transfers between devices  14.2 us (11%)
  matrix products  7.48 us (6%)
  local copies, waits for them, and re-layouts  5.54 us (4%)
  between operations  1.41 us (1%)
    all_to_all x1, blocking collectives, body(): lax.all_to_all(flat.reshape(peers, share, LANES), 'rep', 0, 0, tiled=True)  50.7 us
    all_to_all x1, waiting for transfers between devices, body(): lax.all_to_all(mine, 'rep', 0, 0, tiled=True).reshape(peers * share, LANES)  27 us
    all_to_all x1, waiting for transfers between devices, body(): lax.all_to_all(jnp.swapaxes(pooled[0], 0, 1), 'tab', 0, 0, tiled=True)  12.3 us
    all_to_all x1, waiting for transfers between devices, body(): lax.all_to_all(jnp.swapaxes(d_proj[0], 0, 1), 'tab', 0, 0, tiled=True)  8.59 us
    all_to_all x1, starting transfers between devices, body(): lax.all_to_all(mine, 'rep', 0, 0, tiled=True).reshape(peers * share, LANES)  6.36 us
    all_to_all x1, starting transfers between devices, body(): lax.all_to_all(jnp.swapaxes(d_proj[0], 0, 1), 'tab', 0, 0, tiled=True)  4.3 us
    unnamed x14, local copies, waits for them, and re-layouts  3.95 us
    all_to_all x1, starting transfers between devices, body(): lax.all_to_all(jnp.swapaxes(pooled[0], 0, 1), 'tab', 0, 0, tiled=True)  3.56 us
  transfers between devices with their start and end apart: 3, of which 3 were waited for; matrix products, arithmetic and copies ran while one was open for 5% of the time, Pallas kernels for 0%

profile of v1, /device:TPU:8, one launch (start us, length us, event | category | flops | bytes accessed | tf_op | source)
XLA Modules:
  0.0 128.6 jit_solution(15956570457351459047)
XLA Ops:
  0.6 0.0 copy-start
  0.6 0.0 copy-start.1
  0.6 2.0 %copy.11 = bf16[1,128,8,256]{3,1,2,0:T(8,128)(2,1)} copy(bf16[1,128,8,256]{3,2,1,0:T(8,128)(2,1)} %param.6) | data formatting | bytes 1048576 | tf_op args[0]
  2.7 4.3 %all-to-all-start = ((bf16[8,128,256]{2,1,0:T(8,128)(2,1)}), bf16[8,128,256]{2,1,0:T(8,128)(2,1)S(1)}, u32[]{:S(2)}, u32[]{:S(2)}) async-start(bf16[8,128,256]{2,1,0:T(8,128)(2,1)} %bitcast.36), calls=%async_computation | async-start | bytes 1048576 | tf_op jit(solution)/shard_map/all_to_all | solution.py:23
  7.0 0.0 copy-done
  7.0 0.0 copy-start.2
  7.0 1.7 %copy.9 = bf16[1,128,8,512]{1,3,2,0:T(8,128)(2,1)} copy(bf16[1,128,8,512]{3,2,1,0:T(8,128)(2,1)S(1)} %copy-done) | data formatting | bytes 2097152 | tf_op args[1]
  8.7 0.0 copy-done.1
  8.7 8.6 %all-to-all-done = bf16[8,128,256]{2,1,0:T(8,128)(2,1)S(1)} async-done(((bf16[8,128,256]{2,1,0:T(8,128)(2,1)}), bf16[8,128,256]{2,1,0:T(8,128)(2,1)S(1)}, u32[]{:S(2)}, u32[]{:S(2)}) %all-to-all-start) | async-done | bytes 524320 | tf_op jit(solution)/shard_map/all_to_all | solution.py:23
  17.3 3.6 %all-to-all-start.1 = ((bf16[8,128,512]{1,2,0:T(8,128)(2,1)}), bf16[8,128,512]{1,2,0:T(8,128)(2,1)S(1)}, u32[]{:S(2)}, u32[]{:S(2)}) async-start(bf16[8,128,512]{1,2,0:T(8,128)(2,1)} %bitcast.12), calls=%async_computation.1 | async-start | bytes 2097152 | tf_op jit(solution)/shard_map/all_to_all | solution.py:25
  20.9 0.0 copy-done.2
  20.9 0.1 compare_reduce_fusion.7
  21.0 3.3 %convolution_convert_fusion = f16[512,256]{1,0:T(8,128)(2,1)S(1)} fusion(bf16[1024,256]{1,0:T(8,128)(2,1)S(1)} %bitcast.39, s32[1024]{0:T(1024)S(1)} %bitcast.46, s32[1024]{0:T(1024)S(1)} %bitcast.47, s32[1024]{0:T(1024)S(1)} %bitcast.41, s32[1024]{0:T(1024)S(1)} %bitcast.42, s32[1024]{0:T(1024)S(1)} %bitcast.43, s32[1024]{0:T(1024)S(1)} %bitcast.44, ...), kind=kOutput, calls=%fused_computation.20 | convolution fusion | flops 285343744 | bytes 827392 | tf_op jit(solution)/shard_map/dot_general | solution.py:35
  24.4 0.1 slice_dynamic-update-slice_fusion.3
  24.5 12.3 %all-to-all-done.1 = bf16[8,128,512]{1,2,0:T(8,128)(2,1)S(1)} async-done(((bf16[8,128,512]{1,2,0:T(8,128)(2,1)}), bf16[8,128,512]{1,2,0:T(8,128)(2,1)S(1)}, u32[]{:S(2)}, u32[]{:S(2)}) %all-to-all-start.1) | async-done | bytes 1048608 | tf_op jit(solution)/shard_map/all_to_all | solution.py:25
  36.8 0.4 fusion.9
  37.2 0.0 copy-start.3
  37.3 50.7 %all_to_all.20 = f16[96,24,128]{2,1,0:T(8,128)(2,1)S(1)} all-to-all(f16[96,24,128]{2,1,0:T(8,128)(2,1)S(1)} %bitcast.38), channel_id=1, replica_groups=mesh['tab'=8,'rep'=96] {'rep'}, dimensions={0} | all-to-all | bytes 1179648 | tf_op jit(solution)/shard_map/all_to_all | solution.py:45
  88.1 0.1 convert_reduce_fusion
  88.2 0.9 broadcast_in_dim.22
  89.1 6.4 %all-to-all-start.3 = ((f16[96,24,128]{2,1,0:T(8,128)(2,1)}), f16[96,24,128]{2,1,0:T(8,128)(2,1)S(1)}, u32[]{:S(2)}, u32[]{:S(2)}) async-start(f16[96,24,128]{2,1,0:T(8,128)(2,1)} %broadcast_in_dim.22), calls=%async_computation.3 | async-start | bytes 1179648 | tf_op jit(solution)/shard_map/all_to_all | solution.py:49
  95.5 0.0 copy-done.3
  95.5 0.6 dynamic_slice.8
  96.7 27.0 %all-to-all-done.3 = f16[96,24,128]{2,1,0:T(8,128)(2,1)S(1)} async-done(((f16[96,24,128]{2,1,0:T(8,128)(2,1)}), f16[96,24,128]{2,1,0:T(8,128)(2,1)S(1)}, u32[]{:S(2)}, u32[]{:S(2)}) %all-to-all-start.3) | async-done | bytes 589856 | tf_op jit(solution)/shard_map/all_to_all | solution.py:49
  123.8 0.1 convert_multiply_fusion
  123.9 0.1 slice_bitcast_fusion.1
  123.9 1.4 %fusion.27 = f32[512,512]{1,0:T(8,128)S(1)} fusion(f32[512,128]{1,0:T(8,128)S(1)} %get-tuple-element.12, f32[512,128]{1,0:T(8,128)S(1)} %get-tuple-element.13, bf16[8,512,256]{2,1,0:T(8,128)(2,1)} %param.8, s32[]{:T(128)S(6)} %select_n.21, pred[512]{0:T(512)(128)(4,1)S(1)} %iota_compare_fusion.8), kind=kOutput, calls=%fused_computation.45 | convolution fusion | flops 134873088 | bytes 1835524 | tf_op jit(solution)/shard_map/dot_general | solution.py:64
  125.3 2.3 %fusion.8 = f32[1,512,512]{2,1,0:T(8,128)} fusion(f32[512,512]{1,0:T(8,128)S(1)} %fusion.27, f32[512,128]{1,0:T(8,128)S(1)} %get-tuple-element.12, f32[512,128]{1,0:T(8,128)S(1)} %get-tuple-element.13, bf16[8,512,256]{2,1,0:T(8,128)(2,1)} %param.8, s32[]{:T(128)S(6)} %select_n.21, pred[512]{0:T(512)(128)(4,1)S(1)} %iota_compare_fusion.8), kind=kOutput, calls=%fused_computation.18 | convolution fusion | flops 135266304 | bytes 2884100 | tf_op jit(solution)/shard_map/dot_general | solution.py:66
  127.6 0.9 maximum_select_fusion
  (7 shorter events, 0.2 us)
Async XLA Ops:
  0.6 6.3 %copy-start = (bf16[1,128,8,512]{3,2,1,0:T(8,128)(2,1)S(1)}, bf16[1,128,8,512]{3,2,1,0:T(8,128)(2,1)}, u32[]{:S(2)}) copy-start(bf16[1,128,8,512]{3,2,1,0:T(8,128)(2,1)} %param.7) | copy-start | bytes 3145732
  0.6 8.1 %copy-start.1 = (s32[1,1024,1,8]{1,3,2,0:T(8,128)S(1)}, s32[1,1024,1,8]{1,3,2,0:T(8,128)}, u32[]{:S(2)}) copy-start(s32[1,1024,1,8]{1,3,2,0:T(8,128)} %param.9) | copy-start | bytes 98308
  2.7 14.6 %all-to-all-start = ((bf16[8,128,256]{2,1,0:T(8,128)(2,1)}), bf16[8,128,256]{2,1,0:T(8,128)(2,1)S(1)}, u32[]{:S(2)}, u32[]{:S(2)}) async-start(bf16[8,128,256]{2,1,0:T(8,128)(2,1)} %bitcast.36), calls=%async_computation | async-start | bytes 1048576 | tf_op jit(solution)/shard_map/all_to_all | solution.py:23
  7.0 13.9 %copy-start.2 = (s32[1,1024,1]{1,2,0:T(1,128)S(1)}, s32[1,1024,1]{1,2,0:T(1,128)}, u32[]{:S(2)}) copy-start(s32[1,1024,1]{1,2,0:T(1,128)} %param.10) | copy-start | bytes 12292
  17.3 19.5 %all-to-all-start.1 = ((bf16[8,128,512]{1,2,0:T(8,128)(2,1)}), bf16[8,128,512]{1,2,0:T(8,128)(2,1)S(1)}, u32[]{:S(2)}, u32[]{:S(2)}) async-start(bf16[8,128,512]{1,2,0:T(8,128)(2,1)} %bitcast.12), calls=%async_computation.1 | async-start | bytes 2097152 | tf_op jit(solution)/shard_map/all_to_all | solution.py:25
  37.2 58.2 %copy-start.3 = (s32[8]{0:T(128)S(1)}, s32[8]{0:T(128)}, u32[]{:S(2)}) copy-start(s32[8]{0:T(128)} %param.11) | copy-start | bytes 100
  89.1 34.7 %all-to-all-start.3 = ((f16[96,24,128]{2,1,0:T(8,128)(2,1)}), f16[96,24,128]{2,1,0:T(8,128)(2,1)S(1)}, u32[]{:S(2)}, u32[]{:S(2)}) async-start(f16[96,24,128]{2,1,0:T(8,128)(2,1)} %broadcast_in_dim.22), calls=%async_computation.3 | async-start | bytes 1179648 | tf_op jit(solution)/shard_map/all_to_all | solution.py:49

commit v2 on v1

v2 whole, which is shorter than its diff:
```python
import jax
import jax.numpy as jnp
from jax import lax
from jax.sharding import Mesh, PartitionSpec as P

ROWS = 512
LANES = 128
WIRE = jnp.float16
NEAR = ("zl", "y")
FAR = "zh"
REP = ("zh", "zl", "y")
Y = 8
ZL = 4


def halves(part):
    return [part[:, at : at + LANES] for at in range(0, part.shape[1], LANES)]


def to_all(block, axes, peers):
    return lax.all_to_all(
        jnp.broadcast_to(block[None], (peers,) + block.shape), axes, 0, 0, tiled=True
    )


def body(d_proj, pooled, proj, bag_rows, bag_lengths, dim_blocks):
    tables, widest, width = proj.shape
    group_rows = bag_rows.shape[1]
    bag_size = bag_rows.shape[3]
    near = lax.axis_size(NEAR)
    far = lax.axis_size(FAR)
    table = lax.axis_index("tab")

    both = jnp.concatenate(
        [jnp.swapaxes(d_proj[0], 0, 1), jnp.swapaxes(pooled[0], 0, 1)], axis=2
    )
    got = lax.all_to_all(both, "tab", 0, 0, tiled=True).reshape(group_rows, width + widest)
    samples, pools = got[:, :width], got[:, width:]

    row_ids = jnp.arange(ROWS, dtype=jnp.int32)
    counts = jnp.zeros((ROWS, group_rows), jnp.float32)
    for slot in range(bag_size):
        hit = (bag_rows[0, :, 0, slot][None, :] == row_ids[:, None]) & (
            slot < bag_lengths[0, :, 0]
        )[None, :]
        counts = counts + hit.astype(jnp.float32)
    limit = widest // 16 * lax.dynamic_index_in_dim(dim_blocks, table, 0, keepdims=False)
    live = jnp.arange(widest, dtype=jnp.int32) < limit
    weight = lax.dynamic_index_in_dim(proj, table, 0, keepdims=False)
    weight = jnp.where(live[:, None], weight, jnp.zeros_like(weight))
    counts, weight = lax.optimization_barrier(
        (counts.astype(jnp.bfloat16), jnp.concatenate([weight, weight], axis=1))
    )

    row_sums = jnp.dot(counts, samples, preferred_element_type=jnp.float32)
    outer = lax.dot_general(
        pools, samples, (((0,), (0,)), ((), ())), preferred_element_type=jnp.float32
    )

    flat = jnp.concatenate([piece.astype(WIRE) for piece in halves(row_sums) + halves(outer)], axis=0)
    parts = lax.all_to_all(flat.reshape(near, -1, LANES), NEAR, 0, 0, tiled=True)
    part = jnp.sum(parts.astype(jnp.float32), axis=0)
    part = to_all((part * (1.0 / 32.0)).astype(WIRE), FAR, far)
    total = jnp.sum(part.astype(jnp.float32), axis=0) * (32.0 / 128.0)
    full = to_all(total.astype(WIRE), NEAR, near).reshape(-1, LANES).astype(jnp.float32) * 128.0

    split = width // LANES
    row_total = jnp.concatenate([full[i * ROWS : (i + 1) * ROWS] for i in range(split)], axis=1)
    base = split * ROWS
    proj_grad = jnp.concatenate(
        [full[base + i * widest : base + (i + 1) * widest] for i in range(split)], axis=1
    )
    high = lax.reduce_precision(row_total, 8, 7)
    terms = jnp.concatenate([high, row_total - high], axis=1).astype(jnp.bfloat16)
    emb_grad = lax.dot_general(
        terms, weight, (((1,), (1,)), ((), ())), preferred_element_type=jnp.float32
    )
    proj_grad = jnp.where(live[:, None], proj_grad, 0.0)
    return (emb_grad[None], proj_grad[None])


def solution(mesh):
    tab = mesh.devices.shape[0]
    fine = Mesh(mesh.devices.reshape(tab, -1, ZL, Y), ("tab",) + REP)
    placed = (
        P(REP, "tab", None, None),
        P(REP, "tab", None, None),
        P(),
        P(REP, None, "tab", None),
        P(REP, None, "tab"),
        P(),
    )
    return jax.shard_map(
        body,
        mesh=fine,
        in_specs=placed,
        out_specs=(P("tab", None, None), P("tab", None, None)),
        check_vma=False,
    )
```

time: 129 us -> 105 us (0.81)
  waiting for transfers between devices: 47.9 us -> 15.7 us
  blocking collectives: 50.7 us -> 69.7 us
  starting transfers between devices: 14.2 us -> 4.43 us
  other arithmetic: 1.28 us -> 7.21 us
  matrix products: 7.48 us -> 2.36 us
  local copies, waits for them, and re-layouts: 5.54 us -> 3.64 us
    all_to_all x3 -> x1, waiting for transfers between devices: 47.9 us -> 15.7 us  [body(): lax.all_to_all(both, 'tab', 0, 0, tiled=True)]
    all_to_all x1 -> x3, blocking collectives: 50.7 us -> 69.7 us  [the longest x2 39.6 us: to_all(): lax.all_to_all(jnp.broadcast_to(block[None], (peers,) + block.shape), axe...]
    all_to_all x3 -> x1, starting transfers between devices: 14.2 us -> 4.43 us  [body(): lax.all_to_all(both, 'tab', 0, 0, tiled=True)]
    dot_general x3 -> x2, matrix products: 7.05 us -> 1.88 us  [the longest x1 1.44 us: body(): lax.dot_general(terms, weight, (((1,), (1,)), ((), ())), preferred_elemen...]
    convert_element_type x1 -> x3, other arithmetic: 0.01 us -> 3.32 us  [the longest x1 3.3 us: body(): counts.astype(jnp.bfloat16)]
    concatenate x0 -> x3, other arithmetic: none -> 1.48 us  [the longest x1 1.27 us: body(): jnp.concatenate([jnp.swapaxes(d_proj[0], 0, 1), jnp.swapaxes(pooled[0], 0...]
    unnamed x14 -> x8, local copies, waits for them, and re-layouts: 3.95 us -> 2.69 us
  transfers between devices with their start and end apart: 3 -> 1, of which waited for: 3 -> 1; matrix products, arithmetic and copies ran while one was open for 5% -> 5% of each run, Pallas kernels for 0% -> 0%
where the time goes in v2:
time: 105 us
  blocking collectives  69.7 us (66%)
  waiting for transfers between devices  15.7 us (15%)
  other arithmetic  7.21 us (7%)
  starting transfers between devices  4.43 us (4%)
  local copies, waits for them, and re-layouts  3.64 us (3%)
  matrix products  2.36 us (2%)
  between operations  1.42 us (1%)
    all_to_all x2, blocking collectives, to_all(): lax.all_to_all(jnp.broadcast_to(block[None], (peers,) + block.shape), axe...  39.6 us
    all_to_all x1, blocking collectives, body(): lax.all_to_all(flat.reshape(near, -1, LANES), NEAR, 0, 0, tiled=True)  30.1 us
    all_to_all x1, waiting for transfers between devices, body(): lax.all_to_all(both, 'tab', 0, 0, tiled=True)  15.7 us
    all_to_all x1, starting transfers between devices, body(): lax.all_to_all(both, 'tab', 0, 0, tiled=True)  4.43 us
    convert_element_type x1, other arithmetic, body(): counts.astype(jnp.bfloat16)  3.3 us
    unnamed x8, local copies, waits for them, and re-layouts  2.69 us
  transfers between devices with their start and end apart: 1, of which 1 were waited for; matrix products, arithmetic and copies ran while one was open for 5% of the time, Pallas kernels for 0%

profile of v2, /device:TPU:8, one launch (start us, length us, event | category | flops | bytes accessed | tf_op | source)
XLA Modules:
  0.0 104.5 jit_solution(1717931060354607154)
XLA Ops:
  0.6 1.1 %copy.15 = bf16[1,128,8,256]{3,1,2,0:T(8,128)(2,1)S(1)} copy(bf16[1,128,8,256]{3,2,1,0:T(8,128)(2,1)} %param.6) | data formatting | bytes 1048576 | tf_op args[0]
  1.8 1.5 %copy.14 = bf16[1,128,8,512]{3,1,2,0:T(8,128)(2,1)S(1)} copy(bf16[1,128,8,512]{3,2,1,0:T(8,128)(2,1)} %param.7) | data formatting | bytes 2097152 | tf_op args[1]
  3.3 1.3 %pad_maximum_fusion = bf16[8,128,768]{2,1,0:T(8,128)(2,1)} fusion(bf16[8,128,512]{2,1,0:T(8,128)(2,1)S(1)} %bitcast.31, bf16[8,128,256]{2,1,0:T(8,128)(2,1)S(1)} %bitcast.33), kind=kLoop, calls=%fused_computation.17 | loop fusion | flops 3145728 | bytes 3145728 | tf_op jit(solution)/shard_map/concatenate | solution.py:34
  4.6 0.0 copy-start.2
  4.6 0.0 copy-start.1
  4.6 0.0 copy-start
  4.6 4.4 %all-to-all-start = ((bf16[8,128,768]{2,1,0:T(8,128)(2,1)}), bf16[8,128,768]{2,1,0:T(8,128)(2,1)S(1)}, u32[]{:S(2)}, u32[]{:S(2)}) async-start(bf16[8,128,768]{2,1,0:T(8,128)(2,1)} %pad_maximum_fusion), calls=%async_computation | async-start | bytes 3145728 | tf_op jit(solution)/shard_map/all_to_all | solution.py:37
  9.0 0.0 copy-done.2
  9.0 0.6 dynamic_slice.8
  10.3 0.0 copy-done.1
  10.3 0.1 compare_reduce_fusion.7
  10.4 1.1 %bitcast_select_fusion = bf16[512,256]{1,0:T(8,128)(2,1)S(1)} fusion(bf16[8,512,256]{2,1,0:T(8,128)(2,1)} %param.8, s32[]{:T(128)S(6)} %select_n.21, pred[512]{0:T(512)(128)(4,1)S(1)} %iota_compare_fusion.8), kind=kLoop, calls=%fused_computation.38 | loop fusion | flops 131072 | bytes 524804 | tf_op jit(solution)/shard_map/jit(_where)/select_n | solution.py:50
  11.5 0.0 copy-done
  11.6 3.3 %add_convert_fusion = bf16[512,1024]{1,0:T(8,128)(2,1)S(1)} fusion(s32[1024]{0:T(1024)S(1)} %bitcast.46, s32[1024]{0:T(1024)S(1)} %bitcast.47, s32[1024]{0:T(1024)S(1)} %bitcast.41, s32[1024]{0:T(1024)S(1)} %bitcast.42, s32[1024]{0:T(1024)S(1)} %bitcast.43, s32[1024]{0:T(1024)S(1)} %bitcast.44, s32[1024]{0:T(1024)S(1)} %bitcast.45, s32[1024]{0:T(1024)S(1)} %bitcast.40, ...), kind=kLoop, calls=%fused_computation | loop fusion | flops 16777216 | bytes 1089536 | tf_op jit(solution)/shard_map/convert_element_type | solution.py:52
  14.9 15.7 %all-to-all-done = bf16[8,128,768]{2,1,0:T(8,128)(2,1)S(1)} async-done(((bf16[8,128,768]{2,1,0:T(8,128)(2,1)}), bf16[8,128,768]{2,1,0:T(8,128)(2,1)S(1)}, u32[]{:S(2)}, u32[]{:S(2)}) %all-to-all-start) | async-done | bytes 1572896 | tf_op jit(solution)/shard_map/all_to_all | solution.py:37
  30.6 0.5 convolution_convert_fusion
  31.1 0.4 convolution_convert_fusion.1
  31.5 0.1 fusion.17
  31.7 0.2 pad_maximum_fusion.2
  31.8 30.1 %all_to_all.20 = f16[32,64,128]{2,1,0:T(8,128)(2,1)S(1)} all-to-all(f16[32,64,128]{2,1,0:T(8,128)(2,1)S(1)} %bitcast.32), channel_id=1, replica_groups=mesh['tab'=8,'zh'=3,'zl'=4,'y'=8] {'zl','y'}, dimensions={0} | all-to-all | bytes 1048576 | tf_op jit(solution)/shard_map/all_to_all | solution.py:61
  62.0 0.1 convert_reduce_fusion
  62.1 18.9 %all_to_all.21 = f16[3,64,128]{2,1,0:T(8,128)(2,1)S(1)} all-to-all(f16[3,64,128]{2,1,0:T(8,128)(2,1)S(1)} %broadcast_in_dim.26), channel_id=1, replica_groups=mesh['tab'=8,'zh'=3,'zl'=4,'y'=8] {'zh'}, dimensions={0} | all-to-all | bytes 98304 | tf_op jit(solution)/shard_map/all_to_all | solution.py:21
  81.0 0.1 broadcast_in_dim.27
  81.1 20.7 %all_to_all.22 = f16[32,64,128]{2,1,0:T(8,128)(2,1)S(1)} all-to-all(f16[32,64,128]{2,1,0:T(8,128)(2,1)S(1)} %broadcast_in_dim.27), channel_id=1, replica_groups=mesh['tab'=8,'zh'=3,'zl'=4,'y'=8] {'zl','y'}, dimensions={0} | all-to-all | bytes 1048576 | tf_op jit(solution)/shard_map/all_to_all | solution.py:21
  101.8 0.1 convert_multiply_fusion
  102.0 0.1 fusion.16
  102.1 0.9 maximum_select_fusion
  103.0 0.1 reduce-precision_convert_fusion
  103.1 1.4 %convolution_bitcast_fusion = f32[1,512,512]{2,1,0:T(8,128)} fusion(bf16[512,512]{1,0:T(8,128)(2,1)S(1)} %pad_maximum_fusion.1, bf16[512,256]{1,0:T(8,128)(2,1)S(1)} %get-tuple-element.19, bf16[512,256]{1,0:T(8,128)(2,1)S(1)} %get-tuple-element.18), kind=kOutput, calls=%fused_computation.18 | convolution fusion | flops 269484032 | bytes 2097152 | tf_op jit(solution)/shard_map/dot_general | solution.py:75
  (7 shorter events, 0.1 us)
Async XLA Ops:
  4.6 4.4 %copy-start.2 = (s32[8]{0:T(128)S(1)}, s32[8]{0:T(128)}, u32[]{:S(2)}) copy-start(s32[8]{0:T(128)} %param.11) | copy-start | bytes 100
  4.6 5.7 %copy-start.1 = (s32[1,1024,1]{1,2,0:T(1,128)S(1)}, s32[1,1024,1]{1,2,0:T(1,128)}, u32[]{:S(2)}) copy-start(s32[1,1024,1]{1,2,0:T(1,128)} %param.10) | copy-start | bytes 12292
  4.6 6.9 %copy-start = (s32[1,1024,1,8]{1,3,2,0:T(8,128)S(1)}, s32[1,1024,1,8]{1,3,2,0:T(8,128)}, u32[]{:S(2)}) copy-start(s32[1,1024,1,8]{1,3,2,0:T(8,128)} %param.9) | copy-start | bytes 98308
  4.6 26.0 %all-to-all-start = ((bf16[8,128,768]{2,1,0:T(8,128)(2,1)}), bf16[8,128,768]{2,1,0:T(8,128)(2,1)S(1)}, u32[]{:S(2)}, u32[]{:S(2)}) async-start(bf16[8,128,768]{2,1,0:T(8,128)(2,1)} %pad_maximum_fusion), calls=%async_computation | async-start | bytes 3145728 | tf_op jit(solution)/shard_map/all_to_all | solution.py:37

commit v3 on v2

--- a/solution.py
+++ b/solution.py
@@ -6,7 +6,7 @@
 ROWS = 512
 LANES = 128
 WIRE = jnp.float16
-NEAR = ("zl", "y")
+NEAR = ("y", "zl")
 FAR = "zh"
 REP = ("zh", "zl", "y")
 Y = 8
@@ -60,8 +60,18 @@
     flat = jnp.concatenate([piece.astype(WIRE) for piece in halves(row_sums) + halves(outer)], axis=0)
     parts = lax.all_to_all(flat.reshape(near, -1, LANES), NEAR, 0, 0, tiled=True)
     part = jnp.sum(parts.astype(jnp.float32), axis=0)
-    part = to_all((part * (1.0 / 32.0)).astype(WIRE), FAR, far)
-    total = jnp.sum(part.astype(jnp.float32), axis=0) * (32.0 / 128.0)
+    mine = (part * (1.0 / 32.0)).astype(WIRE)
+    seat = lax.axis_index(FAR)
+    seats = [mine] + [
+        lax.ppermute(mine, FAR, [(i, (i + hop) % far) for i in range(far)]) for hop in range(1, far)
+    ]
+    total = jnp.zeros(mine.shape, jnp.float32)
+    for source in range(far):
+        term = mine
+        for hop in range(1, far):
+            term = jnp.where((seat - hop) % far == source, seats[hop], term)
+        total = total + term.astype(jnp.float32)
+    total = total * (32.0 / 128.0)
     full = to_all(total.astype(WIRE), NEAR, near).reshape(-1, LANES).astype(jnp.float32) * 128.0
 
     split = width // LANES

time: 105 us -> 106 us (level)
  blocking collectives: 69.7 us -> 50.1 us
  starting transfers between devices: 4.43 us -> 18.2 us
  waiting for transfers between devices: 15.7 us -> 23.5 us
    all_to_all x2 -> x1, blocking collectives: 39.6 us -> 20 us  [to_all(): lax.all_to_all(jnp.broadcast_to(block[None], (peers,) + block.shape), axe...]
    ppermute x0 -> x2, starting transfers between devices: none -> 13.8 us  [body(): lax.ppermute(mine, FAR, [(i, (i + hop) % far) for i in range(far)])]
    ppermute x0 -> x2, waiting for transfers between devices: none -> 7.8 us  [body(): lax.ppermute(mine, FAR, [(i, (i + hop) % far) for i in range(far)])]
    unnamed x8 -> x10, local copies, waits for them, and re-layouts: 2.69 us -> 1.71 us
  transfers between devices with their start and end apart: 1 -> 3, of which waited for: 1 -> 2; matrix products, arithmetic and copies ran while one was open for 5% -> 5% of each run, Pallas kernels for 0% -> 0%
where the time goes in v3:
time: 106 us
  blocking collectives  50.1 us (47%)
  waiting for transfers between devices  23.5 us (22%)
  starting transfers between devices  18.2 us (17%)
  other arithmetic  7.22 us (7%)
  local copies, waits for them, and re-layouts  2.65 us (2%)
  matrix products  2.36 us (2%)
  between operations  1.51 us (1%)
    all_to_all x1, blocking collectives, body(): lax.all_to_all(flat.reshape(near, -1, LANES), NEAR, 0, 0, tiled=True)  30.1 us
    all_to_all x1, blocking collectives, to_all(): lax.all_to_all(jnp.broadcast_to(block[None], (peers,) + block.shape), axe...  20 us
    all_to_all x1, waiting for transfers between devices, body(): lax.all_to_all(both, 'tab', 0, 0, tiled=True)  15.7 us
    ppermute x2, starting transfers between devices, body(): lax.ppermute(mine, FAR, [(i, (i + hop) % far) for i in range(far)])  13.8 us
    ppermute x2, waiting for transfers between devices, body(): lax.ppermute(mine, FAR, [(i, (i + hop) % far) for i in range(far)])  7.8 us
    all_to_all x1, starting transfers between devices, body(): lax.all_to_all(both, 'tab', 0, 0, tiled=True)  4.43 us
    convert_element_type x1, other arithmetic, body(): counts.astype(jnp.bfloat16)  3.3 us
  transfers between devices with their start and end apart: 3, of which 2 were waited for; matrix products, arithmetic and copies ran while one was open for 5% of the time, Pallas kernels for 0%

profile of v3, /device:TPU:8, one launch (start us, length us, event | category | flops | bytes accessed | tf_op | source)
XLA Modules:
  0.0 105.5 jit_solution(11826722406497146184)
XLA Ops:
  0.6 0.0 copy-start
  0.6 1.6 %copy.12 = bf16[1,128,8,512]{3,1,2,0:T(8,128)(2,1)S(1)} copy(bf16[1,128,8,512]{3,2,1,0:T(8,128)(2,1)} %param.7) | data formatting | bytes 2097152 | tf_op args[1]
  2.2 0.0 copy-done
  2.2 0.1 copy.13
  2.4 1.3 %pad_maximum_fusion = bf16[8,128,768]{2,1,0:T(8,128)(2,1)} fusion(bf16[8,128,512]{2,1,0:T(8,128)(2,1)S(1)} %bitcast.31, bf16[8,128,256]{2,1,0:T(8,128)(2,1)S(1)} %bitcast.33), kind=kLoop, calls=%fused_computation.17 | loop fusion | flops 3145728 | bytes 3145728 | tf_op jit(solution)/shard_map/concatenate | solution.py:34
  3.6 0.0 copy-start.3
  3.6 0.0 copy-start.2
  3.6 0.0 copy-start.1
  3.6 4.4 %all-to-all-start = ((bf16[8,128,768]{2,1,0:T(8,128)(2,1)}), bf16[8,128,768]{2,1,0:T(8,128)(2,1)S(1)}, u32[]{:S(2)}, u32[]{:S(2)}) async-start(bf16[8,128,768]{2,1,0:T(8,128)(2,1)} %pad_maximum_fusion), calls=%async_computation | async-start | bytes 3145728 | tf_op jit(solution)/shard_map/all_to_all | solution.py:37
  8.1 0.0 copy-done.3
  8.1 0.6 dynamic_slice.8
  9.3 0.0 copy-done.2
  9.3 0.1 compare_reduce_fusion.7
  9.4 1.1 %bitcast_select_fusion = bf16[512,256]{1,0:T(8,128)(2,1)S(1)} fusion(bf16[8,512,256]{2,1,0:T(8,128)(2,1)} %param.8, s32[]{:T(128)S(6)} %select_n.80, pred[512]{0:T(512)(128)(4,1)S(1)} %iota_compare_fusion.8), kind=kLoop, calls=%fused_computation.38 | loop fusion | flops 131072 | bytes 524804 | tf_op jit(solution)/shard_map/jit(_where)/select_n | solution.py:50
  10.6 0.0 copy-done.1
  10.6 3.3 %add_convert_fusion = bf16[512,1024]{1,0:T(8,128)(2,1)S(1)} fusion(s32[1024]{0:T(1024)S(1)} %bitcast.46, s32[1024]{0:T(1024)S(1)} %bitcast.47, s32[1024]{0:T(1024)S(1)} %bitcast.41, s32[1024]{0:T(1024)S(1)} %bitcast.42, s32[1024]{0:T(1024)S(1)} %bitcast.43, s32[1024]{0:T(1024)S(1)} %bitcast.44, s32[1024]{0:T(1024)S(1)} %bitcast.45, s32[1024]{0:T(1024)S(1)} %bitcast.40, ...), kind=kLoop, calls=%fused_computation | loop fusion | flops 16777216 | bytes 1089536 | tf_op jit(solution)/shard_map/convert_element_type | solution.py:52
  13.9 15.7 %all-to-all-done = bf16[8,128,768]{2,1,0:T(8,128)(2,1)S(1)} async-done(((bf16[8,128,768]{2,1,0:T(8,128)(2,1)}), bf16[8,128,768]{2,1,0:T(8,128)(2,1)S(1)}, u32[]{:S(2)}, u32[]{:S(2)}) %all-to-all-start) | async-done | bytes 1572896 | tf_op jit(solution)/shard_map/all_to_all | solution.py:37
  29.6 0.5 convolution_convert_fusion
  30.1 0.4 convolution_convert_fusion.1
  30.6 0.1 fusion.17
  30.7 0.2 pad_maximum_fusion.2
  30.9 30.1 %all_to_all.15 = f16[32,64,128]{2,1,0:T(8,128)(2,1)S(1)} all-to-all(f16[32,64,128]{2,1,0:T(8,128)(2,1)S(1)} %bitcast.32), channel_id=1, replica_groups=mesh['tab'=8,'zh'=3,'zl'=4,'y'=8] {'y','zl'}, dimensions={0} | all-to-all | bytes 1048576 | tf_op jit(solution)/shard_map/all_to_all | solution.py:61
  61.0 0.1 convert_reduce_fusion
  61.1 11.9 %collective-permute-start = (f16[64,128]{1,0:T(8,128)(2,1)S(1)}, f16[64,128]{1,0:T(8,128)(2,1)S(1)}, u32[]{:S(2)}, u32[]{:S(2)}) collective-permute-start(f16[64,128]{1,0:T(8,128)(2,1)S(1)} %multiply_convert_fusion.1), channel_id=1, source_target_pairs={{0,64},{32,0},{64,32},{1,65},{33,1},{65,33},{2,66},{34,2},{66,34},... | collective-permute-start | bytes 49160 | tf_op jit(solution)/shard_map/ppermute | solution.py:66
  73.0 1.9 %collective-permute-start.1 = (f16[64,128]{1,0:T(8,128)(2,1)S(1)}, f16[64,128]{1,0:T(8,128)(2,1)S(1)}, u32[]{:S(2)}, u32[]{:S(2)}) collective-permute-start(f16[64,128]{1,0:T(8,128)(2,1)S(1)} %multiply_convert_fusion.1), channel_id=1, source_target_pairs={{0,32},{32,64},{64,0},{1,33},{33,65},{65,1},{2,34},{34,66},{66,2},... | collective-permute-start | bytes 49160 | tf_op jit(solution)/shard_map/ppermute | solution.py:66
  74.9 0.0 collective-permute-done
  74.9 7.8 %collective-permute-done.1 = f16[64,128]{1,0:T(8,128)(2,1)S(1)} collective-permute-done((f16[64,128]{1,0:T(8,128)(2,1)S(1)}, f16[64,128]{1,0:T(8,128)(2,1)S(1)}, u32[]{:S(2)}, u32[]{:S(2)}) %collective-permute-start.1) | collective-permute-done | bytes 16416 | tf_op jit(solution)/shard_map/ppermute | solution.py:66
  82.8 0.1 broadcast_in_dim.24
  82.9 20.0 %all_to_all.16 = f16[32,64,128]{2,1,0:T(8,128)(2,1)S(1)} all-to-all(f16[32,64,128]{2,1,0:T(8,128)(2,1)S(1)} %broadcast_in_dim.24), channel_id=1, replica_groups=mesh['tab'=8,'zh'=3,'zl'=4,'y'=8] {'y','zl'}, dimensions={0} | all-to-all | bytes 1048576 | tf_op jit(solution)/shard_map/all_to_all | solution.py:21
  102.8 0.1 convert_multiply_fusion
  103.0 0.1 fusion.16
  103.1 0.1 reduce-precision_convert_fusion
  103.2 0.9 maximum_select_fusion
  104.1 1.4 %convolution_bitcast_fusion = f32[1,512,512]{2,1,0:T(8,128)} fusion(bf16[512,512]{1,0:T(8,128)(2,1)S(1)} %pad_maximum_fusion.1, bf16[512,256]{1,0:T(8,128)(2,1)S(1)} %get-tuple-element.19, bf16[512,256]{1,0:T(8,128)(2,1)S(1)} %get-tuple-element.18), kind=kOutput, calls=%fused_computation.18 | convolution fusion | flops 269484032 | bytes 2097152 | tf_op jit(solution)/shard_map/dot_general | solution.py:85
  (5 shorter events, 0.1 us)
Async XLA Ops:
  0.6 1.6 %copy-start = (bf16[1,128,8,256]{3,2,1,0:T(8,128)(2,1)S(1)}, bf16[1,128,8,256]{3,2,1,0:T(8,128)(2,1)}, u32[]{:S(2)}) copy-start(bf16[1,128,8,256]{3,2,1,0:T(8,128)(2,1)} %param.6) | copy-start | bytes 1572868
  3.6 4.4 %copy-start.3 = (s32[8]{0:T(128)S(1)}, s32[8]{0:T(128)}, u32[]{:S(2)}) copy-start(s32[8]{0:T(128)} %param.11) | copy-start | bytes 100
  3.6 5.7 %copy-start.2 = (s32[1,1024,1]{1,2,0:T(1,128)S(1)}, s32[1,1024,1]{1,2,0:T(1,128)}, u32[]{:S(2)}) copy-start(s32[1,1024,1]{1,2,0:T(1,128)} %param.10) | copy-start | bytes 12292
  3.6 7.0 %copy-start.1 = (s32[1,1024,1,8]{1,3,2,0:T(8,128)S(1)}, s32[1,1024,1,8]{1,3,2,0:T(8,128)}, u32[]{:S(2)}) copy-start(s32[1,1024,1,8]{1,3,2,0:T(8,128)} %param.9) | copy-start | bytes 98308
  3.6 26.0 %all-to-all-start = ((bf16[8,128,768]{2,1,0:T(8,128)(2,1)}), bf16[8,128,768]{2,1,0:T(8,128)(2,1)S(1)}, u32[]{:S(2)}, u32[]{:S(2)}) async-start(bf16[8,128,768]{2,1,0:T(8,128)(2,1)} %pad_maximum_fusion), calls=%async_computation | async-start | bytes 3145728 | tf_op jit(solution)/shard_map/all_to_all | solution.py:37
  61.1 13.8 %collective-permute-start = (f16[64,128]{1,0:T(8,128)(2,1)S(1)}, f16[64,128]{1,0:T(8,128)(2,1)S(1)}, u32[]{:S(2)}, u32[]{:S(2)}) collective-permute-start(f16[64,128]{1,0:T(8,128)(2,1)S(1)} %multiply_convert_fusion.1), channel_id=1, source_target_pairs={{0,64},{32,0},{64,32},{1,65},{33,1},{65,33},{2,66},{34,2},{66,34},... | collective-permute-start | bytes 49160 | tf_op jit(solution)/shard_map/ppermute | solution.py:66
  73.0 9.8 %collective-permute-start.1 = (f16[64,128]{1,0:T(8,128)(2,1)S(1)}, f16[64,128]{1,0:T(8,128)(2,1)S(1)}, u32[]{:S(2)}, u32[]{:S(2)}) collective-permute-start(f16[64,128]{1,0:T(8,128)(2,1)S(1)} %multiply_convert_fusion.1), channel_id=1, source_target_pairs={{0,32},{32,64},{64,0},{1,33},{33,65},{65,1},{2,34},{34,66},{66,2},... | collective-permute-start | bytes 49160 | tf_op jit(solution)/shard_map/ppermute | solution.py:66

commit v4 on v2

--- a/solution.py
+++ b/solution.py
@@ -1,15 +1,18 @@
 import jax
 import jax.numpy as jnp
 from jax import lax
+from jax.experimental import pallas as pl
+from jax.experimental.pallas import tpu as pltpu
 from jax.sharding import Mesh, PartitionSpec as P
 
 ROWS = 512
 LANES = 128
 WIRE = jnp.float16
-NEAR = ("zl", "y")
+NEAR = ("y", "zl")
 FAR = "zh"
 REP = ("zh", "zl", "y")
 Y = 8
+BLOCK = 32
 ZL = 4
 
 
@@ -23,6 +26,82 @@
     )
 
 
+def by_table(d_proj, pooled):
+    samples, tables, width = d_proj.shape
+    widest = pooled.shape[2]
+    rows = BLOCK * tables
+
+    def kernel(d_ref, p_ref, out_ref):
+        to = lax.broadcasted_iota(jnp.int32, (rows, rows), 0)
+        source = lax.broadcasted_iota(jnp.int32, (rows, rows), 1)
+        swap = (source == (to % BLOCK) * tables + to // BLOCK).astype(jnp.bfloat16)
+        for block in range(samples // BLOCK):
+            at = slice(block * BLOCK, (block + 1) * BLOCK)
+            for ref, left in ((d_ref, 0), (p_ref, width)):
+                wide = ref.shape[2]
+                moved = jnp.dot(
+                    swap, ref[at].reshape(rows, wide), preferred_element_type=jnp.float32
+                )
+                out_ref[:, at, left : left + wide] = moved.astype(out_ref.dtype).reshape(
+                    tables, BLOCK, wide
+                )
+
+    return pl.pallas_call(
+        kernel,
+        in_specs=[pl.BlockSpec(memory_space=pltpu.VMEM)] * 2,
+        out_specs=pl.BlockSpec(memory_space=pltpu.VMEM),
+        out_shape=jax.ShapeDtypeStruct((tables, samples, width + widest), d_proj.dtype),
+        compiler_params=pltpu.CompilerParams(vmem_limit_bytes=60 * 2**20),
+        cost_estimate=pl.CostEstimate(
+            flops=2 * samples * tables * rows * (width + widest),
+            transcendentals=0,
+            bytes_accessed=4 * samples * tables * (width + widest),
+        ),
+    )(d_proj, pooled)
+
+
+def finish(full, weight, limit):
+    quarters, rows, lanes = full.shape
+    widest, width = weight.shape
+    tile = 256
+
+    def kernel(limit_ref, full_ref, weight_ref, emb_ref, proj_ref):
+        sums = full_ref[...] * 128.0
+        row_total = jnp.concatenate([sums[0], sums[1]], axis=1)
+        high = row_total.astype(jnp.bfloat16)
+        low = (row_total - high.astype(jnp.float32)).astype(jnp.bfloat16)
+        last = (((1,), (1,)), ((), ()))
+        emb_ref[0] = lax.dot_general(
+            high, weight_ref[...], last, preferred_element_type=jnp.float32
+        ) + lax.dot_general(low, weight_ref[...], last, preferred_element_type=jnp.float32)
+        row = lax.broadcasted_iota(jnp.int32, (tile, 1), 0) + pl.program_id(0) * tile
+        proj_ref[0] = jnp.where(
+            row < limit_ref[0], jnp.concatenate([sums[2], sums[3]], axis=1), 0.0
+        )
+
+    return pl.pallas_call(
+        kernel,
+        grid=(rows // tile,),
+        in_specs=[
+            pl.BlockSpec(memory_space=pltpu.SMEM),
+            pl.BlockSpec((quarters, tile, lanes), lambda i: (0, i, 0)),
+            pl.BlockSpec((widest, width), lambda i: (0, 0)),
+        ],
+        out_specs=[
+            pl.BlockSpec((1, tile, widest), lambda i: (0, i, 0)),
+            pl.BlockSpec((1, tile, width), lambda i: (0, i, 0)),
+        ],
+        out_shape=[
+            jax.ShapeDtypeStruct((1, rows, widest), jnp.float32),
+            jax.ShapeDtypeStruct((1, widest, width), jnp.float32),
+        ],
+        compiler_params=pltpu.CompilerParams(vmem_limit_bytes=16 * 2**20),
+        cost_estimate=pl.CostEstimate(
+            flops=4 * rows * widest * width, transcendentals=0, bytes_accessed=8 * rows * widest
+        ),
+    )(limit[None], full, weight)
+
+
 def body(d_proj, pooled, proj, bag_rows, bag_lengths, dim_blocks):
     tables, widest, width = proj.shape
     group_rows = bag_rows.shape[1]
@@ -31,10 +110,7 @@
     far = lax.axis_size(FAR)
     table = lax.axis_index("tab")
 
-    both = jnp.concatenate(
-        [jnp.swapaxes(d_proj[0], 0, 1), jnp.swapaxes(pooled[0], 0, 1)], axis=2
-    )
-    got = lax.all_to_all(both, "tab", 0, 0, tiled=True).reshape(group_rows, width + widest)
+    got = lax.all_to_all(by_table(d_proj[0], pooled[0]), "tab", 0, 0, tiled=True).reshape(group_rows, width + widest)
     samples, pools = got[:, :width], got[:, width:]
 
     row_ids = jnp.arange(ROWS, dtype=jnp.int32)
@@ -48,9 +124,7 @@
     live = jnp.arange(widest, dtype=jnp.int32) < limit
     weight = lax.dynamic_index_in_dim(proj, table, 0, keepdims=False)
     weight = jnp.where(live[:, None], weight, jnp.zeros_like(weight))
-    counts, weight = lax.optimization_barrier(
-        (counts.astype(jnp.bfloat16), jnp.concatenate([weight, weight], axis=1))
-    )
+    counts, weight = lax.optimization_barrier((counts.astype(jnp.bfloat16), weight))
 
     row_sums = jnp.dot(counts, samples, preferred_element_type=jnp.float32)
     outer = lax.dot_general(
@@ -62,21 +136,9 @@
     part = jnp.sum(parts.astype(jnp.float32), axis=0)
     part = to_all((part * (1.0 / 32.0)).astype(WIRE), FAR, far)
     total = jnp.sum(part.astype(jnp.float32), axis=0) * (32.0 / 128.0)
-    full = to_all(total.astype(WIRE), NEAR, near).reshape(-1, LANES).astype(jnp.float32) * 128.0
-
-    split = width // LANES
-    row_total = jnp.concatenate([full[i * ROWS : (i + 1) * ROWS] for i in range(split)], axis=1)
-    base = split * ROWS
-    proj_grad = jnp.concatenate(
-        [full[base + i * widest : base + (i + 1) * widest] for i in range(split)], axis=1
-    )
-    high = lax.reduce_precision(row_total, 8, 7)
-    terms = jnp.concatenate([high, row_total - high], axis=1).astype(jnp.bfloat16)
-    emb_grad = lax.dot_general(
-        terms, weight, (((1,), (1,)), ((), ())), preferred_element_type=jnp.float32
-    )
-    proj_grad = jnp.where(live[:, None], proj_grad, 0.0)
-    return (emb_grad[None], proj_grad[None])
+    full = to_all(total.astype(WIRE), NEAR, near).astype(jnp.float32)
+    emb_grad, proj_grad = finish(full.reshape(-1, ROWS, LANES), weight, limit)
+    return (emb_grad, proj_grad)
 
 
 def solution(mesh):

time: 105 us -> 103 us (0.981)
  Pallas kernels: 0 us -> 4.78 us
  local copies, waits for them, and re-layouts: 3.64 us -> 0.86 us
  other arithmetic: 7.21 us -> 4.86 us
  matrix products: 2.36 us -> 0.92 us
    pallas_call x0 -> x2, Pallas kernels: none -> 4.78 us  [the longest x1 3.12 us: by_table(): pl.pallas_call(kernel, in_specs=[pl.BlockSpec(memory_space=pltpu.VMEM)] *...]
    unnamed x8 -> x6, local copies, waits for them, and re-layouts: 2.69 us -> 0.01 us
    dot_general x1 -> x0, matrix products: 1.44 us -> none  [body(): lax.dot_general(terms, weight, (((1,), (1,)), ((), ())), preferred_elemen...]
    concatenate x2 -> x0, other arithmetic: 1.3 us -> none  [the longest x1 1.27 us: body(): jnp.concatenate([jnp.swapaxes(d_proj[0], 0, 1), jnp.swapaxes(pooled[0], 0...]
where the time goes in v4:
time: 103 us; the launch traced here: 102 us
  blocking collectives  69.2 us (67%)
  waiting for transfers between devices  15.8 us (15%)
  other arithmetic  4.86 us (5%)
  Pallas kernels  4.78 us (5%)
  starting transfers between devices  4.43 us (4%)
  between operations  1.39 us (1%)
    all_to_all x2, blocking collectives, to_all(): lax.all_to_all(jnp.broadcast_to(block[None], (peers,) + block.shape), axe...  39.1 us
    all_to_all x1, blocking collectives, body(): lax.all_to_all(flat.reshape(near, -1, LANES), NEAR, 0, 0, tiled=True)  30.1 us
    all_to_all x1, waiting for transfers between devices, body(): lax.all_to_all(by_table(d_proj[0], pooled[0]), 'tab', 0, 0, tiled=True)  15.8 us
    all_to_all x1, starting transfers between devices, body(): lax.all_to_all(by_table(d_proj[0], pooled[0]), 'tab', 0, 0, tiled=True)  4.43 us
    convert_element_type x1, other arithmetic, body(): counts.astype(jnp.bfloat16)  3.3 us
    pallas_call x1, Pallas kernels, by_table(): pl.pallas_call(kernel, in_specs=[pl.BlockSpec(memory_space=pltpu.VMEM)] *...  3.12 us
  transfers between devices with their start and end apart: 1, of which 1 were waited for; matrix products, arithmetic and copies ran while one was open for 5% of the time, Pallas kernels for 0%

profile of v4, /device:TPU:8, one launch (start us, length us, event | category | flops | bytes accessed | tf_op | source)
XLA Modules:
  0.0 102.2 jit_solution(3021903035391936716)
XLA Ops:
  0.6 3.1 %shard_map.77 = bf16[8,128,768]{2,1,0:T(8,128)(2,1)} custom-call(bf16[128,8,256]{2,1,0:T(8,128)(2,1)} %bitcast.25, bf16[128,8,512]{2,1,0:T(8,128)(2,1)} %bitcast.24), custom_call_target="tpu_custom_call" | custom-call | flops 402653184 | bytes 3145728 | tf_op jit(solution)/shard_map/pallas_call | solution.py:49
  3.8 0.0 copy-start.2
  3.8 0.0 copy-start.1
  3.8 0.0 copy-start
  3.8 4.4 %all-to-all-start = ((bf16[8,128,768]{2,1,0:T(8,128)(2,1)}), bf16[8,128,768]{2,1,0:T(8,128)(2,1)S(1)}, u32[]{:S(2)}, u32[]{:S(2)}) async-start(bf16[8,128,768]{2,1,0:T(8,128)(2,1)} %shard_map.77), calls=%async_computation | async-start | bytes 3145728 | tf_op jit(solution)/shard_map/all_to_all | solution.py:113
  8.2 0.0 copy-done.2
  8.2 0.6 dynamic_slice.8
  9.4 0.0 copy-done.1
  9.5 0.1 compare_reduce_fusion.7
  9.6 0.0 copy-done
  9.6 1.1 %bitcast_select_fusion.weight_ref = bf16[512,256]{1,0:T(8,128)(2,1)S(1)} fusion(bf16[8,512,256]{2,1,0:T(8,128)(2,1)} %param.8, s32[]{:T(128)S(6)} %select_n.10, pred[512]{0:T(512)(128)(4,1)S(1)} %iota_compare_fusion.8), kind=kLoop, calls=%fused_computation.25 | loop fusion | flops 131072 | bytes 524804 | tf_op jit(solution)/shard_map/jit(_where)/select_n | solution.py:126
  10.7 3.3 %add_convert_fusion = bf16[512,1024]{1,0:T(8,128)(2,1)S(1)} fusion(s32[1024]{0:T(1024)S(1)} %bitcast.32, s32[1024]{0:T(1024)S(1)} %bitcast.33, s32[1024]{0:T(1024)S(1)} %bitcast.27, s32[1024]{0:T(1024)S(1)} %bitcast.28, s32[1024]{0:T(1024)S(1)} %bitcast.29, s32[1024]{0:T(1024)S(1)} %bitcast.30, s32[1024]{0:T(1024)S(1)} %bitcast.31, s32[1024]{0:T(1024)S(1)} %bitcast.26, ...), kind=kLoop, calls=%fused_computation | loop fusion | flops 16777216 | bytes 1089536 | tf_op jit(solution)/shard_map/convert_element_type | solution.py:127
  14.0 15.8 %all-to-all-done = bf16[8,128,768]{2,1,0:T(8,128)(2,1)S(1)} async-done(((bf16[8,128,768]{2,1,0:T(8,128)(2,1)}), bf16[8,128,768]{2,1,0:T(8,128)(2,1)S(1)}, u32[]{:S(2)}, u32[]{:S(2)}) %all-to-all-start) | async-done | bytes 1572896 | tf_op jit(solution)/shard_map/all_to_all | solution.py:113
  29.8 0.5 convolution_convert_fusion
  30.3 0.4 convolution_convert_fusion.1
  30.7 0.1 fusion.11
  30.8 0.2 pad_maximum_fusion
  31.0 30.1 %all_to_all.20 = f16[32,64,128]{2,1,0:T(8,128)(2,1)S(1)} all-to-all(f16[32,64,128]{2,1,0:T(8,128)(2,1)S(1)} %bitcast.21), channel_id=1, replica_groups=mesh['tab'=8,'zh'=3,'zl'=4,'y'=8] {'y','zl'}, dimensions={0} | all-to-all | bytes 1048576 | tf_op jit(solution)/shard_map/all_to_all | solution.py:135
  61.1 0.1 convert_reduce_fusion
  61.2 18.9 %all_to_all.21 = f16[3,64,128]{2,1,0:T(8,128)(2,1)S(1)} all-to-all(f16[3,64,128]{2,1,0:T(8,128)(2,1)S(1)} %broadcast_in_dim.13), channel_id=1, replica_groups=mesh['tab'=8,'zh'=3,'zl'=4,'y'=8] {'zh'}, dimensions={0} | all-to-all | bytes 98304 | tf_op jit(solution)/shard_map/all_to_all | solution.py:24
  80.1 0.1 broadcast_in_dim.14
  80.3 20.2 %all_to_all.22 = f16[32,64,128]{2,1,0:T(8,128)(2,1)S(1)} all-to-all(f16[32,64,128]{2,1,0:T(8,128)(2,1)S(1)} %broadcast_in_dim.14), channel_id=1, replica_groups=mesh['tab'=8,'zh'=3,'zl'=4,'y'=8] {'y','zl'}, dimensions={0} | all-to-all | bytes 1048576 | tf_op jit(solution)/shard_map/all_to_all | solution.py:24
  100.5 0.1 bitcast_convert_fusion.full_ref
  100.6 1.7 %shard_map.78 = (f32[1,512,512]{2,1,0:T(8,128)}, f32[1,512,256]{2,1,0:T(8,128)}) custom-call(s32[1]{0:T(128)} %mul_shard_map.6.limit_ref, f32[4,512,128]{2,1,0:T(8,128)S(1)} %bitcast_convert_fusion.full_ref, bf16[512,256]{1,0:T(8,128)(2,1)S(1)} %bitcast_select_fusion.weight_ref), custom_call_target="tpu_custom_call" | custom-call | flops 268435456 | bytes 2097152 | tf_op jit(solution)/shard_map/pallas_call | solution.py:82
  (6 shorter events, 0.1 us)
Async XLA Ops:
  3.8 4.4 %copy-start.2 = (s32[8]{0:T(128)S(1)}, s32[8]{0:T(128)}, u32[]{:S(2)}) copy-start(s32[8]{0:T(128)} %param.11) | copy-start | bytes 100
  3.8 5.7 %copy-start.1 = (s32[1,1024,1]{1,2,0:T(1,128)S(1)}, s32[1,1024,1]{1,2,0:T(1,128)}, u32[]{:S(2)}) copy-start(s32[1,1024,1]{1,2,0:T(1,128)} %param.10) | copy-start | bytes 12292
  3.8 5.8 %copy-start = (s32[1,1024,1,8]{1,3,2,0:T(8,128)S(1)}, s32[1,1024,1,8]{1,3,2,0:T(8,128)}, u32[]{:S(2)}) copy-start(s32[1,1024,1,8]{1,3,2,0:T(8,128)} %param.9) | copy-start | bytes 98308
  3.8 26.0 %all-to-all-start = ((bf16[8,128,768]{2,1,0:T(8,128)(2,1)}), bf16[8,128,768]{2,1,0:T(8,128)(2,1)S(1)}, u32[]{:S(2)}, u32[]{:S(2)}) async-start(bf16[8,128,768]{2,1,0:T(8,128)(2,1)} %shard_map.77), calls=%async_computation | async-start | bytes 3145728 | tf_op jit(solution)/shard_map/all_to_all | solution.py:113

commit v5 on v4

--- a/solution.py
+++ b/solution.py
@@ -6,7 +6,6 @@
 from jax.sharding import Mesh, PartitionSpec as P
 
 ROWS = 512
-LANES = 128
 WIRE = jnp.float16
 NEAR = ("y", "zl")
 FAR = "zh"
@@ -14,10 +13,6 @@
 Y = 8
 BLOCK = 32
 ZL = 4
-
-
-def halves(part):
-    return [part[:, at : at + LANES] for at in range(0, part.shape[1], LANES)]
 
 
 def to_all(block, axes, peers):
@@ -31,11 +26,13 @@
     widest = pooled.shape[2]
     rows = BLOCK * tables
 
+    step = BLOCK * 2
+
     def kernel(d_ref, p_ref, out_ref):
         to = lax.broadcasted_iota(jnp.int32, (rows, rows), 0)
         source = lax.broadcasted_iota(jnp.int32, (rows, rows), 1)
         swap = (source == (to % BLOCK) * tables + to // BLOCK).astype(jnp.bfloat16)
-        for block in range(samples // BLOCK):
+        for block in range(step // BLOCK):
             at = slice(block * BLOCK, (block + 1) * BLOCK)
             for ref, left in ((d_ref, 0), (p_ref, width)):
                 wide = ref.shape[2]
@@ -48,8 +45,12 @@
 
     return pl.pallas_call(
         kernel,
-        in_specs=[pl.BlockSpec(memory_space=pltpu.VMEM)] * 2,
-        out_specs=pl.BlockSpec(memory_space=pltpu.VMEM),
+        grid=(samples // step,),
+        in_specs=[
+            pl.BlockSpec((step, tables, width), lambda i: (i, 0, 0)),
+            pl.BlockSpec((step, tables, widest), lambda i: (i, 0, 0)),
+        ],
+        out_specs=pl.BlockSpec((tables, step, width + widest), lambda i: (0, i, 0)),
         out_shape=jax.ShapeDtypeStruct((tables, samples, width + widest), d_proj.dtype),
         compiler_params=pltpu.CompilerParams(vmem_limit_bytes=60 * 2**20),
         cost_estimate=pl.CostEstimate(
@@ -61,13 +62,13 @@
 
 
 def finish(full, weight, limit):
-    quarters, rows, lanes = full.shape
-    widest, width = weight.shape
+    kinds, rows, width = full.shape
+    widest = weight.shape[0]
     tile = 256
 
     def kernel(limit_ref, full_ref, weight_ref, emb_ref, proj_ref):
         sums = full_ref[...] * 128.0
-        row_total = jnp.concatenate([sums[0], sums[1]], axis=1)
+        row_total = sums[0]
         high = row_total.astype(jnp.bfloat16)
         low = (row_total - high.astype(jnp.float32)).astype(jnp.bfloat16)
         last = (((1,), (1,)), ((), ()))
@@ -75,16 +76,14 @@
             high, weight_ref[...], last, preferred_element_type=jnp.float32
         ) + lax.dot_general(low, weight_ref[...], last, preferred_element_type=jnp.float32)
         row = lax.broadcasted_iota(jnp.int32, (tile, 1), 0) + pl.program_id(0) * tile
-        proj_ref[0] = jnp.where(
-            row < limit_ref[0], jnp.concatenate([sums[2], sums[3]], axis=1), 0.0
-        )
+        proj_ref[0] = jnp.where(row < limit_ref[0], sums[1], 0.0)
 
     return pl.pallas_call(
         kernel,
         grid=(rows // tile,),
         in_specs=[
             pl.BlockSpec(memory_space=pltpu.SMEM),
-            pl.BlockSpec((quarters, tile, lanes), lambda i: (0, i, 0)),
+            pl.BlockSpec((kinds, tile, width), lambda i: (0, i, 0)),
             pl.BlockSpec((widest, width), lambda i: (0, 0)),
         ],
         out_specs=[
@@ -131,13 +130,13 @@
         pools, samples, (((0,), (0,)), ((), ())), preferred_element_type=jnp.float32
     )
 
-    flat = jnp.concatenate([piece.astype(WIRE) for piece in halves(row_sums) + halves(outer)], axis=0)
-    parts = lax.all_to_all(flat.reshape(near, -1, LANES), NEAR, 0, 0, tiled=True)
+    flat = jnp.concatenate([row_sums.astype(WIRE), outer.astype(WIRE)], axis=0)
+    parts = lax.all_to_all(flat.reshape(near, -1, width), NEAR, 0, 0, tiled=True)
     part = jnp.sum(parts.astype(jnp.float32), axis=0)
     part = to_all((part * (1.0 / 32.0)).astype(WIRE), FAR, far)
     total = jnp.sum(part.astype(jnp.float32), axis=0) * (32.0 / 128.0)
     full = to_all(total.astype(WIRE), NEAR, near).astype(jnp.float32)
-    emb_grad, proj_grad = finish(full.reshape(-1, ROWS, LANES), weight, limit)
+    emb_grad, proj_grad = finish(full.reshape(2, ROWS, width), weight, limit)
     return (emb_grad, proj_grad)
 
 

time: 103 us -> 102 us (level)
  no operation moved by 1% of the time
where the time goes in v5:
time: 102 us
  blocking collectives  69.2 us (68%)
  waiting for transfers between devices  15.8 us (15%)
  other arithmetic  4.81 us (5%)
  Pallas kernels  4.44 us (4%)
  starting transfers between devices  4.44 us (4%)
  between operations  1.39 us (1%)
    all_to_all x2, blocking collectives, to_all(): lax.all_to_all(jnp.broadcast_to(block[None], (peers,) + block.shape), axe...  39.1 us
    all_to_all x1, blocking collectives, body(): lax.all_to_all(flat.reshape(near, -1, width), NEAR, 0, 0, tiled=True)  30.1 us
    all_to_all x1, waiting for transfers between devices, body(): lax.all_to_all(by_table(d_proj[0], pooled[0]), 'tab', 0, 0, tiled=True)  15.8 us
    all_to_all x1, starting transfers between devices, body(): lax.all_to_all(by_table(d_proj[0], pooled[0]), 'tab', 0, 0, tiled=True)  4.44 us
    convert_element_type x1, other arithmetic, body(): counts.astype(jnp.bfloat16)  3.3 us
    pallas_call x1, Pallas kernels, by_table(): pl.pallas_call(kernel, grid=(samples // step,), in_specs=[pl.BlockSpec((s...  2.79 us
  transfers between devices with their start and end apart: 1, of which 1 were waited for; matrix products, arithmetic and copies ran while one was open for 5% of the time, Pallas kernels for 0%

profile of v5, /device:TPU:8, one launch (start us, length us, event | category | flops | bytes accessed | tf_op | source)
XLA Modules:
  0.0 101.7 jit_solution(15034066961019121380)
XLA Ops:
  0.6 2.8 %shard_map.77 = bf16[8,128,768]{2,1,0:T(8,128)(2,1)} custom-call(bf16[128,8,256]{2,1,0:T(8,128)(2,1)} %bitcast.25, bf16[128,8,512]{2,1,0:T(8,128)(2,1)} %bitcast.24), custom_call_target="tpu_custom_call" | custom-call | flops 402653184 | bytes 3145728 | tf_op jit(solution)/shard_map/pallas_call | solution.py:46
  3.4 0.0 copy-start.2
  3.4 0.0 copy-start.1
  3.4 0.0 copy-start
  3.4 4.4 %all-to-all-start = ((bf16[8,128,768]{2,1,0:T(8,128)(2,1)}), bf16[8,128,768]{2,1,0:T(8,128)(2,1)S(1)}, u32[]{:S(2)}, u32[]{:S(2)}) async-start(bf16[8,128,768]{2,1,0:T(8,128)(2,1)} %shard_map.77), calls=%async_computation | async-start | bytes 3145728 | tf_op jit(solution)/shard_map/all_to_all | solution.py:112
  7.9 0.0 copy-done.2
  7.9 0.6 dynamic_slice.8
  9.1 0.0 copy-done.1
  9.1 0.1 compare_reduce_fusion.7
  9.2 0.0 copy-done
  9.3 1.1 %bitcast_select_fusion.weight_ref = bf16[512,256]{1,0:T(8,128)(2,1)S(1)} fusion(bf16[8,512,256]{2,1,0:T(8,128)(2,1)} %param.8, s32[]{:T(128)S(6)} %select_n.10, pred[512]{0:T(512)(128)(4,1)S(1)} %iota_compare_fusion.8), kind=kLoop, calls=%fused_computation.25 | loop fusion | flops 131072 | bytes 524804 | tf_op jit(solution)/shard_map/jit(_where)/select_n | solution.py:125
  10.4 3.3 %add_convert_fusion = bf16[512,1024]{1,0:T(8,128)(2,1)S(1)} fusion(s32[1024]{0:T(1024)S(1)} %bitcast.32, s32[1024]{0:T(1024)S(1)} %bitcast.33, s32[1024]{0:T(1024)S(1)} %bitcast.27, s32[1024]{0:T(1024)S(1)} %bitcast.28, s32[1024]{0:T(1024)S(1)} %bitcast.29, s32[1024]{0:T(1024)S(1)} %bitcast.30, s32[1024]{0:T(1024)S(1)} %bitcast.31, s32[1024]{0:T(1024)S(1)} %bitcast.26, ...), kind=kLoop, calls=%fused_computation | loop fusion | flops 16777216 | bytes 1089536 | tf_op jit(solution)/shard_map/convert_element_type | solution.py:126
  13.7 15.8 %all-to-all-done = bf16[8,128,768]{2,1,0:T(8,128)(2,1)S(1)} async-done(((bf16[8,128,768]{2,1,0:T(8,128)(2,1)}), bf16[8,128,768]{2,1,0:T(8,128)(2,1)S(1)}, u32[]{:S(2)}, u32[]{:S(2)}) %all-to-all-start) | async-done | bytes 1572896 | tf_op jit(solution)/shard_map/all_to_all | solution.py:112
  29.5 0.5 convolution_convert_fusion
  29.9 0.4 convolution_convert_fusion.1
  30.4 0.1 pad_maximum_fusion
  30.5 30.1 %all_to_all.20 = f16[32,32,256]{2,1,0:T(8,128)(2,1)S(1)} all-to-all(f16[32,32,256]{2,1,0:T(8,128)(2,1)S(1)} %bitcast.21), channel_id=1, replica_groups=mesh['tab'=8,'zh'=3,'zl'=4,'y'=8] {'y','zl'}, dimensions={0} | all-to-all | bytes 1048576 | tf_op jit(solution)/shard_map/all_to_all | solution.py:134
  60.6 0.1 convert_reduce_fusion
  60.7 18.9 %all_to_all.21 = f16[3,32,256]{2,1,0:T(8,128)(2,1)S(1)} all-to-all(f16[3,32,256]{2,1,0:T(8,128)(2,1)S(1)} %broadcast_in_dim.13), channel_id=1, replica_groups=mesh['tab'=8,'zh'=3,'zl'=4,'y'=8] {'zh'}, dimensions={0} | all-to-all | bytes 98304 | tf_op jit(solution)/shard_map/all_to_all | solution.py:19
  79.6 0.1 broadcast_in_dim.14
  79.7 20.2 %all_to_all.22 = f16[32,32,256]{2,1,0:T(8,128)(2,1)S(1)} all-to-all(f16[32,32,256]{2,1,0:T(8,128)(2,1)S(1)} %broadcast_in_dim.14), channel_id=1, replica_groups=mesh['tab'=8,'zh'=3,'zl'=4,'y'=8] {'y','zl'}, dimensions={0} | all-to-all | bytes 1048576 | tf_op jit(solution)/shard_map/all_to_all | solution.py:19
  99.9 0.1 bitcast_convert_fusion.full_ref
  100.0 1.7 %shard_map.78 = (f32[1,512,512]{2,1,0:T(8,128)}, f32[1,512,256]{2,1,0:T(8,128)}) custom-call(s32[1]{0:T(128)} %mul_shard_map.6.limit_ref, f32[2,512,256]{2,1,0:T(8,128)S(1)} %bitcast_convert_fusion.full_ref, bf16[512,256]{1,0:T(8,128)(2,1)S(1)} %bitcast_select_fusion.weight_ref), custom_call_target="tpu_custom_call" | custom-call | flops 268435456 | bytes 2097152 | tf_op jit(solution)/shard_map/pallas_call | solution.py:81
  (6 shorter events, 0.1 us)
Async XLA Ops:
  3.4 4.5 %copy-start.2 = (s32[8]{0:T(128)S(1)}, s32[8]{0:T(128)}, u32[]{:S(2)}) copy-start(s32[8]{0:T(128)} %param.11) | copy-start | bytes 100
  3.4 5.7 %copy-start.1 = (s32[1,1024,1]{1,2,0:T(1,128)S(1)}, s32[1,1024,1]{1,2,0:T(1,128)}, u32[]{:S(2)}) copy-start(s32[1,1024,1]{1,2,0:T(1,128)} %param.10) | copy-start | bytes 12292
  3.4 5.8 %copy-start = (s32[1,1024,1,8]{1,3,2,0:T(8,128)S(1)}, s32[1,1024,1,8]{1,3,2,0:T(8,128)}, u32[]{:S(2)}) copy-start(s32[1,1024,1,8]{1,3,2,0:T(8,128)} %param.9) | copy-start | bytes 98308
  3.4 26.0 %all-to-all-start = ((bf16[8,128,768]{2,1,0:T(8,128)(2,1)}), bf16[8,128,768]{2,1,0:T(8,128)(2,1)S(1)}, u32[]{:S(2)}, u32[]{:S(2)}) async-start(bf16[8,128,768]{2,1,0:T(8,128)(2,1)} %shard_map.77), calls=%async_computation | async-start | bytes 3145728 | tf_op jit(solution)/shard_map/all_to_all | solution.py:112

commit v6 on v5

--- a/solution.py
+++ b/solution.py
@@ -31,7 +31,8 @@
     def kernel(d_ref, p_ref, out_ref):
         to = lax.broadcasted_iota(jnp.int32, (rows, rows), 0)
         source = lax.broadcasted_iota(jnp.int32, (rows, rows), 1)
-        swap = (source == (to % BLOCK) * tables + to // BLOCK).astype(jnp.bfloat16)
+        sample, table = to & (BLOCK - 1), lax.shift_right_logical(to, BLOCK.bit_length() - 1)
+        swap = (source == sample * tables + table).astype(jnp.bfloat16)
         for block in range(step // BLOCK):
             at = slice(block * BLOCK, (block + 1) * BLOCK)
             for ref, left in ((d_ref, 0), (p_ref, width)):

time: 102 us -> 102 us (level)
  no operation moved by 1% of the time
where the time goes in v6:
time: 102 us
  blocking collectives  69.2 us (68%)
  waiting for transfers between devices  15.8 us (15%)
  other arithmetic  4.81 us (5%)
  Pallas kernels  4.44 us (4%)
  starting transfers between devices  4.44 us (4%)
  between operations  1.39 us (1%)
    all_to_all x2, blocking collectives, to_all(): lax.all_to_all(jnp.broadcast_to(block[None], (peers,) + block.shape), axe...  39.1 us
    all_to_all x1, blocking collectives, body(): lax.all_to_all(flat.reshape(near, -1, width), NEAR, 0, 0, tiled=True)  30.1 us
    all_to_all x1, waiting for transfers between devices, body(): lax.all_to_all(by_table(d_proj[0], pooled[0]), 'tab', 0, 0, tiled=True)  15.8 us
    all_to_all x1, starting transfers between devices, body(): lax.all_to_all(by_table(d_proj[0], pooled[0]), 'tab', 0, 0, tiled=True)  4.44 us
    convert_element_type x1, other arithmetic, body(): counts.astype(jnp.bfloat16)  3.3 us
    pallas_call x1, Pallas kernels, by_table(): pl.pallas_call(kernel, grid=(samples // step,), in_specs=[pl.BlockSpec((s...  2.79 us
  transfers between devices with their start and end apart: 1, of which 1 were waited for; matrix products, arithmetic and copies ran while one was open for 5% of the time, Pallas kernels for 0%

profile of v6, /device:TPU:8, one launch (start us, length us, event | category | flops | bytes accessed | tf_op | source)
XLA Modules:
  0.0 101.7 jit_solution(15466557198652160844)
XLA Ops:
  0.6 2.8 %shard_map.77 = bf16[8,128,768]{2,1,0:T(8,128)(2,1)} custom-call(bf16[128,8,256]{2,1,0:T(8,128)(2,1)} %bitcast.25, bf16[128,8,512]{2,1,0:T(8,128)(2,1)} %bitcast.24), custom_call_target="tpu_custom_call" | custom-call | flops 402653184 | bytes 3145728 | tf_op jit(solution)/shard_map/pallas_call | solution.py:47
  3.4 0.0 copy-start.2
  3.4 0.0 copy-start.1
  3.4 0.0 copy-start
  3.4 4.4 %all-to-all-start = ((bf16[8,128,768]{2,1,0:T(8,128)(2,1)}), bf16[8,128,768]{2,1,0:T(8,128)(2,1)S(1)}, u32[]{:S(2)}, u32[]{:S(2)}) async-start(bf16[8,128,768]{2,1,0:T(8,128)(2,1)} %shard_map.77), calls=%async_computation | async-start | bytes 3145728 | tf_op jit(solution)/shard_map/all_to_all | solution.py:113
  7.9 0.0 copy-done.2
  7.9 0.6 dynamic_slice.8
  9.1 0.0 copy-done.1
  9.1 0.1 compare_reduce_fusion.7
  9.2 0.0 copy-done
  9.3 1.1 %bitcast_select_fusion.weight_ref = bf16[512,256]{1,0:T(8,128)(2,1)S(1)} fusion(bf16[8,512,256]{2,1,0:T(8,128)(2,1)} %param.8, s32[]{:T(128)S(6)} %select_n.10, pred[512]{0:T(512)(128)(4,1)S(1)} %iota_compare_fusion.8), kind=kLoop, calls=%fused_computation.25 | loop fusion | flops 131072 | bytes 524804 | tf_op jit(solution)/shard_map/jit(_where)/select_n | solution.py:126
  10.4 3.3 %add_convert_fusion = bf16[512,1024]{1,0:T(8,128)(2,1)S(1)} fusion(s32[1024]{0:T(1024)S(1)} %bitcast.32, s32[1024]{0:T(1024)S(1)} %bitcast.33, s32[1024]{0:T(1024)S(1)} %bitcast.27, s32[1024]{0:T(1024)S(1)} %bitcast.28, s32[1024]{0:T(1024)S(1)} %bitcast.29, s32[1024]{0:T(1024)S(1)} %bitcast.30, s32[1024]{0:T(1024)S(1)} %bitcast.31, s32[1024]{0:T(1024)S(1)} %bitcast.26, ...), kind=kLoop, calls=%fused_computation | loop fusion | flops 16777216 | bytes 1089536 | tf_op jit(solution)/shard_map/convert_element_type | solution.py:127
  13.7 15.8 %all-to-all-done = bf16[8,128,768]{2,1,0:T(8,128)(2,1)S(1)} async-done(((bf16[8,128,768]{2,1,0:T(8,128)(2,1)}), bf16[8,128,768]{2,1,0:T(8,128)(2,1)S(1)}, u32[]{:S(2)}, u32[]{:S(2)}) %all-to-all-start) | async-done | bytes 1572896 | tf_op jit(solution)/shard_map/all_to_all | solution.py:113
  29.5 0.5 convolution_convert_fusion
  29.9 0.4 convolution_convert_fusion.1
  30.4 0.1 pad_maximum_fusion
  30.5 30.1 %all_to_all.20 = f16[32,32,256]{2,1,0:T(8,128)(2,1)S(1)} all-to-all(f16[32,32,256]{2,1,0:T(8,128)(2,1)S(1)} %bitcast.21), channel_id=1, replica_groups=mesh['tab'=8,'zh'=3,'zl'=4,'y'=8] {'y','zl'}, dimensions={0} | all-to-all | bytes 1048576 | tf_op jit(solution)/shard_map/all_to_all | solution.py:135
  60.6 0.1 convert_reduce_fusion
  60.7 18.9 %all_to_all.21 = f16[3,32,256]{2,1,0:T(8,128)(2,1)S(1)} all-to-all(f16[3,32,256]{2,1,0:T(8,128)(2,1)S(1)} %broadcast_in_dim.13), channel_id=1, replica_groups=mesh['tab'=8,'zh'=3,'zl'=4,'y'=8] {'zh'}, dimensions={0} | all-to-all | bytes 98304 | tf_op jit(solution)/shard_map/all_to_all | solution.py:19
  79.6 0.1 broadcast_in_dim.14
  79.7 20.2 %all_to_all.22 = f16[32,32,256]{2,1,0:T(8,128)(2,1)S(1)} all-to-all(f16[32,32,256]{2,1,0:T(8,128)(2,1)S(1)} %broadcast_in_dim.14), channel_id=1, replica_groups=mesh['tab'=8,'zh'=3,'zl'=4,'y'=8] {'y','zl'}, dimensions={0} | all-to-all | bytes 1048576 | tf_op jit(solution)/shard_map/all_to_all | solution.py:19
  99.9 0.1 bitcast_convert_fusion.full_ref
  100.0 1.7 %shard_map.78 = (f32[1,512,512]{2,1,0:T(8,128)}, f32[1,512,256]{2,1,0:T(8,128)}) custom-call(s32[1]{0:T(128)} %mul_shard_map.6.limit_ref, f32[2,512,256]{2,1,0:T(8,128)S(1)} %bitcast_convert_fusion.full_ref, bf16[512,256]{1,0:T(8,128)(2,1)S(1)} %bitcast_select_fusion.weight_ref), custom_call_target="tpu_custom_call" | custom-call | flops 268435456 | bytes 2097152 | tf_op jit(solution)/shard_map/pallas_call | solution.py:82
  (6 shorter events, 0.1 us)
Async XLA Ops:
  3.4 4.5 %copy-start.2 = (s32[8]{0:T(128)S(1)}, s32[8]{0:T(128)}, u32[]{:S(2)}) copy-start(s32[8]{0:T(128)} %param.11) | copy-start | bytes 100
  3.4 5.7 %copy-start.1 = (s32[1,1024,1]{1,2,0:T(1,128)S(1)}, s32[1,1024,1]{1,2,0:T(1,128)}, u32[]{:S(2)}) copy-start(s32[1,1024,1]{1,2,0:T(1,128)} %param.10) | copy-start | bytes 12292
  3.4 5.8 %copy-start = (s32[1,1024,1,8]{1,3,2,0:T(8,128)S(1)}, s32[1,1024,1,8]{1,3,2,0:T(8,128)}, u32[]{:S(2)}) copy-start(s32[1,1024,1,8]{1,3,2,0:T(8,128)} %param.9) | copy-start | bytes 98308
  3.4 26.0 %all-to-all-start = ((bf16[8,128,768]{2,1,0:T(8,128)(2,1)}), bf16[8,128,768]{2,1,0:T(8,128)(2,1)S(1)}, u32[]{:S(2)}, u32[]{:S(2)}) async-start(bf16[8,128,768]{2,1,0:T(8,128)(2,1)} %shard_map.77), calls=%async_computation | async-start | bytes 3145728 | tf_op jit(solution)/shard_map/all_to_all | solution.py:113
